TPU v7x, 32 devices: a whole 2x2x4 slice. The times are simulated.
32 devices in a mesh: groups: 2 (over x), gx: 4 (over y, core), yz: 4 (over z).
Axes of the slice: x: 2, y: 2, z: 4, core: 2. Of those that a mesh axis runs over, the one named last changes fastest.
Arguments:
- hidden: bfloat16 [64, 16384], P(('groups', 'yz'), 'gx'), parts along dimension 0, may hold values from -24 to 24
- norm_gain: bfloat16 [16384], P('gx'), may hold values from 0.099609375 to 1.8984375
- w_query: bfloat16 [16384, 16384], P('gx', 'yz'), may hold values from -1 to 1
- w_key: bfloat16 [16384, 1024], P('gx', 'yz'), may hold values from -4 to 4
- w_value: bfloat16 [16384, 1024], P('gx', 'yz'), may hold values from -0.046875 to 0.046875
- w_out: bfloat16 [16384, 16384], P('yz', 'gx'), may hold values from -0.046875 to 0.046875
- key_cache: bfloat16 [64, 2048, 1024], P(('groups', 'gx'), None, 'yz'), parts along dimension 0, may hold values from -256 to 256
- value_cache: bfloat16 [64, 2048, 1024], P(('groups', 'gx'), None, 'yz'), parts along dimension 0, may hold values from -6 to 6
- cache_lengths: int32 [64], P(('groups', 'gx')), parts along dimension 0, may hold values from 128 to 2047, as said below
- positions: int32 [64], P(('groups', 'gx')), parts along dimension 0, may hold values from 2048 to 4095
Outputs:
- updated: bfloat16 [64, 16384], P(('groups', 'yz'), 'gx'), parts along dimension 0
There are 2 independent parts, one for each index of `groups`. A program takes and returns all parts, laid end to end along the dimension named above; an argument that names none is the same for every part. Nothing has to cross between parts.
Inputs may be any that keep to these rules, and one draw needn't show every extreme that they name: Slots 0 to cache_lengths - 1 of a row are filled; some row has 2047 filled slots and some row 128.
All inputs are finite; a program needn't handle non-finite values.
Results may differ from a plain program's by a relative error of at most 0.011.
Values may be sent and summed in bfloat16 or wider, within the bound.
A program may use at most 192 MiB of HBM per device.

v0:
```python
import jax
import jax.numpy as jnp
from jax import lax
from jax.sharding import PartitionSpec as P

D = 16384
HD = 128


def rotate(vectors, positions):
    half_size = vectors.shape[-1] // 2
    counter = jnp.arange(half_size, dtype=jnp.float32)
    frequency = jnp.power(jnp.float32(500000.0), -2.0 * counter / vectors.shape[-1])
    angles = positions.astype(jnp.float32)[:, None] * frequency[None, :]
    cosine = jnp.cos(angles)[:, None, :]
    sine_part = jnp.sin(angles)[:, None, :]
    lower_half = vectors[..., :half_size]
    upper_half = vectors[..., half_size:]
    return jnp.concatenate(
        [
            lower_half * cosine - upper_half * sine_part,
            upper_half * cosine + lower_half * sine_part,
        ],
        axis=-1,
    )


def attend(queries, new_key, new_value, keys, values, lengths):
    inv_root = queries.shape[-1] ** (-0.5)
    scores = (
        jnp.einsum("rkge,rcke->rkgc", queries, keys, preferred_element_type=jnp.float32) * inv_root
    )
    fresh = (
        jnp.einsum("rkge,rke->rkg", queries, new_key, preferred_element_type=jnp.float32) * inv_root
    )
    slots = jnp.arange(keys.shape[1], dtype=jnp.int32)
    valid = (slots[None, :] < lengths[:, None])[:, None, None, :]
    masked = jnp.where(valid, scores, -jnp.inf)
    highest = jnp.maximum(jnp.max(masked, axis=-1), fresh)
    weights = jnp.where(valid, jnp.exp(masked - highest[..., None]), 0.0)
    own_weight = jnp.exp(fresh - highest)
    total = jnp.sum(weights, axis=-1) + own_weight
    probs = (weights / total[..., None]).astype(jnp.bfloat16)
    own_prob = (own_weight / total).astype(jnp.bfloat16)
    mixed = jnp.einsum("rkgc,rcke->rkge", probs, values, preferred_element_type=jnp.float32)
    mixed = (
        mixed
        + own_prob.astype(jnp.float32)[..., None] * new_value.astype(jnp.float32)[:, :, None, :]
    )
    return mixed.astype(jnp.bfloat16)


def per_device(
    hidden,
    norm_gain,
    w_query,
    w_key,
    w_value,
    w_out,
    key_cache,
    value_cache,
    cache_lengths,
    positions,
):
    gathered = lax.all_gather(hidden, "yz", axis=0, tiled=True)
    widened = gathered.astype(jnp.float32)
    squares = jnp.sum(widened * widened, axis=1)
    scaled = (widened * norm_gain.astype(jnp.float32)[None, :]).astype(jnp.bfloat16)
    partial_terms = jnp.concatenate(
        [
            jnp.dot(scaled, w_query, preferred_element_type=jnp.float32),
            jnp.dot(scaled, w_key, preferred_element_type=jnp.float32),
            jnp.dot(scaled, w_value, preferred_element_type=jnp.float32),
        ],
        axis=1,
    )
    local_rows = key_cache.shape[0]
    summed, square_sum = lax.psum((partial_terms, squares), "gx")
    first_row = lax.axis_index("gx") * local_rows
    summed = lax.dynamic_slice_in_dim(summed, first_row, local_rows, 0)
    square_sum = lax.dynamic_slice_in_dim(square_sum, first_row, local_rows, 0)
    inverse = lax.rsqrt(square_sum / D + 1e-05)[:, None]
    query_width = w_query.shape[1]
    key_width = w_key.shape[1]
    kv_local = key_width // HD
    group_size = query_width // key_width
    q_part = summed[:, :query_width] * inverse
    k_part = summed[:, query_width : query_width + key_width] * inverse
    v_part = summed[:, query_width + key_width :] * inverse
    queries = rotate(q_part.reshape(local_rows, kv_local * group_size, HD), positions).astype(
        jnp.bfloat16
    )
    queries = queries.reshape(local_rows, kv_local, group_size, HD)
    new_keys = rotate(k_part.reshape(local_rows, kv_local, HD), positions).astype(jnp.bfloat16)
    new_values = v_part.reshape(local_rows, kv_local, HD).astype(jnp.bfloat16)
    slot_count = key_cache.shape[1]
    keys = key_cache.reshape(local_rows, slot_count, kv_local, HD)
    values = value_cache.reshape(local_rows, slot_count, kv_local, HD)
    mixed = attend(queries, new_keys, new_values, keys, values, cache_lengths)
    flat_heads = mixed.reshape(local_rows, query_width)
    all_rows = lax.all_gather(flat_heads, "gx", axis=0, tiled=True)
    out_sum = lax.psum_scatter(
        jnp.dot(all_rows, w_out, preferred_element_type=jnp.float32),
        "yz",
        scatter_dimension=0,
        tiled=True,
    )
    return (hidden.astype(jnp.float32) + out_sum).astype(jnp.bfloat16)


def solution(mesh):
    in_specs = (
        P(("groups", "yz"), "gx"),
        P("gx"),
        P("gx", "yz"),
        P("gx", "yz"),
        P("gx", "yz"),
        P("yz", "gx"),
        P(("groups", "gx"), None, "yz"),
        P(("groups", "gx"), None, "yz"),
        P(("groups", "gx")),
        P(("groups", "gx")),
    )
    out_specs = P(("groups", "yz"), "gx")
    return jax.shard_map(
        per_device, mesh=mesh, in_specs=in_specs, out_specs=out_specs, check_vma=False
    )
```

profile of v0, /device:TPU:0, one launch (start us, length us, event | category | flops | bytes accessed | tf_op | source)
XLA Modules:
  0.0 138.0 jit_solution(15378169891413231771)
XLA Ops:
  6.5 0.0 copy-start
  6.5 0.0 all-reduce.2.cloned.1.call-start
  6.5 0.0 copy-start.2
  6.5 0.8 convert_element_type.54
  7.4 16.0 %all_gather.6 = bf16[32,4096]{1,0:T(8,128)(2,1)S(1)} all-gather(bf16[8,4096]{1,0:T(8,128)(2,1)} %param.10), channel_id=1, replica_groups=mesh['groups'=2,'gx'=4,'yz'=4] {'yz'}, dimensions={0}, use_global_device_ids=true | all-gather | bytes 327680 | tf_op jit(solution)/shard_map/all_gather | solution.py:65
  23.4 0.0 copy-done
  23.4 0.4 fusion.27
  23.8 0.0 copy-done.2
  23.8 0.4 fusion.25
  24.2 0.0 copy-start.5
  24.2 0.0 copy-start.4
  24.2 13.5 %fusion.29 = f32[32,4096]{1,0:T(8,128)S(1)} fusion(bf16[4096,4096]{1,0:T(8,128)(2,1)} %param.12, bf16[32,4096]{1,0:T(8,128)(2,1)S(1)} %all_gather.6, f32[4096]{0:T(1024)S(1)} %convert_element_type.54), kind=kOutput, calls=%fused_computation.24 | convolution fusion | flops 1074135040 | bytes 34357248 | tf_op jit(solution)/shard_map/dot_general | solution.py:71
  37.8 0.9 pad_maximum_fusion
  38.6 0.0 all-reduce.2.cloned.1.call-update
  38.6 0.0 reduce-scatter.2.cloned.1.call-start
  38.7 0.2 fusion.24
  38.9 0.0 copy-done.5
  38.9 0.0 copy-done.4
  38.9 0.1 iota_compare_fusion
  39.0 5.7 %psum.15 = f32[32]{0:T(128)S(1)} all-reduce(f32[32]{0:T(128)S(1)} %fusion.24), channel_id=1, replica_groups=mesh['groups'=2,'gx'=4,'yz'=4] {'gx'}, use_global_device_ids=true, to_apply=%region_2.0 | all-reduce | flops 32 | bytes 256 | tf_op jit(solution)/shard_map/psum | solution.py:78
  44.7 0.1 add_rsqrt_fusion
  44.7 0.1 multiply_cosine_fusion
  44.9 29.0 %all-reduce.2.cloned.1.call-done = f32[32,4608]{1,0:T(8,128)} async-done(((f32[32,4608]{1,0:T(8,128)}), f32[32,4608]{1,0:T(8,128)}) %all-reduce.2.cloned.1.call-update) | async-done | bytes 589840 | tf_op jit(solution)/shard_map/psum | solution.py:78
  73.9 0.8 fusion.37
  74.7 1.0 fusion.31
  75.7 0.1 subtract_convert_fusion
  75.8 0.1 subtract_convert_fusion.1
  75.9 0.1 maximum_bitcast_fusion
  76.0 0.2 fusion.32
  76.2 5.8 %fusion.43 = (f32[8,2,16]{2,1,0:T(2,128)S(1)}, f32[8,2,16,2048]{3,2,1,0:T(8,128)S(1)}) fusion(bf16[8,2,16,64]{3,2,1,0:T(8,128)(2,1)S(1)} %bitcast.52, bf16[8,2,16,64]{3,2,1,0:T(8,128)(2,1)S(1)} %bitcast.50, pred[8,2048]{1,0:T(8,128)(4,1)S(1)} %iota_compare_fusion, bf16[8,2048,256]{2,1,0:T(8,128)(2,1)} %param.16), kind=kOutput, calls=%fused_computation.56 | convolution fusion | flops 135921408 | bytes 10568704 | tf_op jit(solution)/shard_map/rkge,rcke->rkgc/dot_general | solution.py:31
  82.0 0.6 fusion.12
  82.6 4.8 %fusion.16 = bf16[8,2,16,128]{3,2,1,0:T(8,128)(2,1)S(1)} fusion(f32[8,2,16,2048]{3,2,1,0:T(8,128)S(1)} %get-tuple-element.16, f32[8,2,16]{2,1,0:T(2,128)S(1)} %get-tuple-element.10, f32[8,2,16]{2,1,0:T(2,128)S(1)} %multiply_maximum_fusion, pred[8,2048]{1,0:T(8,128)(4,1)S(1)} %iota_compare_fusion, f32[8,2,128]{2,1,0:T(2,128)S(1)} %copy.15, ...), kind=kOutput, calls=%fused_computation.12 | convolution fusion | flops 136413184 | bytes 10578944 | tf_op jit(solution)/shard_map/rkgc,rcke->rkge/dot_general | solution.py:45
  87.5 5.8 %all_gather.7 = bf16[32,4096]{1,0:T(8,128)(2,1)S(1)} all-gather(bf16[8,4096]{1,0:T(8,128)(2,1)S(1)} %bitcast.53), channel_id=1, replica_groups=mesh['groups'=2,'gx'=4,'yz'=4] {'gx'}, dimensions={0}, use_global_device_ids=true | all-gather | bytes 327680 | tf_op jit(solution)/shard_map/all_gather | solution.py:101
  93.3 0.0 copy-start.3
  93.3 0.0 copy-start.1
  93.3 14.5 %fusion.44 = f32[32,4096]{1,0:T(8,128)} fusion(bf16[32,4096]{1,0:T(8,128)(2,1)S(1)} %all_gather.7, bf16[4096,4096]{1,0:T(8,128)(2,1)} %param.15), kind=kOutput, calls=%fused_computation.57 | convolution fusion | flops 1073741824 | bytes 34340864 | tf_op jit(solution)/shard_map/dot_general | solution.py:103
  107.7 0.0 reduce-scatter.2.cloned.1.call-update
  107.8 21.8 %reduce-scatter.2.cloned.1.call-done = f32[8,4096]{1,0:T(8,128)} async-done(((f32[32,4096]{1,0:T(8,128)}), f32[8,4096]{1,0:T(8,128)}) %reduce-scatter.2.cloned.1.call-update) | async-done | bytes 131088 | tf_op jit(solution)/shard_map/reduce_scatter | solution.py:102
  129.6 0.0 copy-done.3
  129.6 1.5 %add_convert_fusion = bf16[8,4096]{1,0:T(8,128)(2,1)} fusion(f32[8,4096]{1,0:T(8,128)} %reduce-scatter.2.cloned.1.call-done, bf16[8,4096]{1,0:T(8,128)(2,1)S(1)} %copy-done.3), kind=kLoop, calls=%fused_computation.27 | loop fusion | flops 98304 | bytes 262144 | tf_op jit(solution)/shard_map/convert_element_type | solution.py:108
  131.1 0.0 copy-done.1
  (8 shorter events, 0.1 us)
Async XLA Ops:
  6.5 16.8 %copy-start = (bf16[4096,256]{1,0:T(8,128)(2,1)S(1)}, bf16[4096,256]{1,0:T(8,128)(2,1)}, u32[]{:S(2)}) copy-start(bf16[4096,256]{1,0:T(8,128)(2,1)} %param.13) | copy-start | bytes 6291460
  6.5 67.4 %all-reduce.2.cloned.1.call-start = ((), (), s32[]{:S(2)}) async-start(), calls=%async_computation.1 | async-start | bytes 1179648 | tf_op jit(solution)/shard_map/psum | solution.py:78
  6.5 17.2 %copy-start.2 = (bf16[4096,256]{1,0:T(8,128)(2,1)S(1)}, bf16[4096,256]{1,0:T(8,128)(2,1)}, u32[]{:S(2)}) copy-start(bf16[4096,256]{1,0:T(8,128)(2,1)} %param.14) | copy-start | bytes 6291460
  24.2 14.7 %copy-start.5 = (s32[8]{0:T(128)S(1)}, s32[8]{0:T(128)}, u32[]{:S(2)}) copy-start(s32[8]{0:T(128)} %param.19) | copy-start | bytes 100
  24.2 14.7 %copy-start.4 = (s32[8]{0:T(128)S(1)}, s32[8]{0:T(128)}, u32[]{:S(2)}) copy-start(s32[8]{0:T(128)} %param.18) | copy-start | bytes 100
  38.6 90.9 %reduce-scatter.2.cloned.1.call-start = ((), (), s32[]{:S(2)}) async-start(), calls=%async_computation.2 | async-start | bytes 655360 | tf_op jit(solution)/shard_map/reduce_scatter | solution.py:102
  93.3 36.3 %copy-start.3 = (bf16[8,4096]{1,0:T(8,128)(2,1)S(1)}, bf16[8,4096]{1,0:T(8,128)(2,1)}, u32[]{:S(2)}) copy-start(bf16[8,4096]{1,0:T(8,128)(2,1)} %param.10) | copy-start | bytes 196612
  93.3 37.8 %copy-start.1 = (bf16[4096,256]{1,0:T(8,128)(2,1)S(1)}, bf16[4096,256]{1,0:T(8,128)(2,1)}, u32[]{:S(2)}) copy-start(bf16[4096,256]{1,0:T(8,128)(2,1)} %param.13) | copy-start | bytes 6291460
Sparse Core Ops, SparseCore 0:
  38.8 35.0 all-reduce.1
  107.9 21.6 reduce-scatter.1
where the time goes:
time: 138 us
  waiting for transfers between devices  50.9 us (37%)
  matrix products  39.6 us (29%)
  blocking collectives  27.4 us (20%)
  between operations  13.5 us (10%)
  other arithmetic  6.35 us (5%)
    psum x1, waiting for transfers between devices, per_device(): summed, square_sum = lax.psum((partial_terms, squares), 'gx')  29 us
    reduce_scatter x1, waiting for transfers between devices, per_device(): lax.psum_scatter(jnp.dot(all_rows, w_out, preferred_element_type=jnp.floa...  21.8 us
    all_gather x1, blocking collectives, per_device(): gathered = lax.all_gather(hidden, 'yz', axis=0, tiled=True)  16 us
    dot_general x1, matrix products, per_device(): jnp.dot(all_rows, w_out, preferred_element_type=jnp.float32)  14.5 us
    dot_general x1, matrix products, per_device(): jnp.dot(scaled, w_query, preferred_element_type=jnp.float32)  13.5 us
    dot_general x1, matrix products, attend(): jnp.einsum('rkge,rcke->rkgc', queries, keys, preferred_element_type=jnp.f...  5.8 us
    all_gather x1, blocking collectives, per_device(): all_rows = lax.all_gather(flat_heads, 'gx', axis=0, tiled=True)  5.79 us
    psum x1, blocking collectives, per_device(): summed, square_sum = lax.psum((partial_terms, squares), 'gx')  5.67 us
  transfers between devices with their start and end apart: 2, of which 2 were waited for; matrix products, arithmetic and copies ran while one was open for 0% of the time, Pallas kernels for 0%

commit v1 on v0

v1 whole, which is shorter than its diff:
```python
import functools

import jax
import jax.numpy as jnp
from jax import lax
from jax.experimental import pallas as pl
from jax.experimental.pallas import tpu as pltpu
from jax.sharding import PartitionSpec as P

D = 16384
HD = 128
MESH = pl.DeviceIdType.MESH
F32 = jnp.float32
BF16 = jnp.bfloat16


def kernel(
    n_gx,
    n_yz,
    q_chunk,
    o_chunk,
    hidden,
    gain,
    w_query,
    w_key,
    w_value,
    w_out,
    key_cache,
    value_cache,
    lengths,
    cosine,
    sine,
    out,
    w_slots,
    wk_buf,
    wv_buf,
    k_buf,
    v_buf,
    x_all,
    scaled,
    sq_own,
    sq_recv,
    p_own,
    p_send,
    p_recv,
    q_rows,
    k_rows,
    v_rows,
    a_send,
    a_all,
    a_wide,
    attended,
    o_own,
    o_send,
    o_recv,
    wq_sem,
    wo_sem,
    wkv_sem,
    kc_sem,
    vc_sem,
    x_own_sem,
    x_ssem,
    x_rsem,
    sq_ssem,
    sq_rsem,
    p_ssem,
    p_rsem,
    a_ssem,
    a_rsem,
    o_ssem,
    o_rsem,
):
    gx = lax.axis_index("gx")
    yz = lax.axis_index("yz")
    q_width = w_query.shape[1]
    k_width = w_key.shape[1]
    depth = w_query.shape[0]
    o_depth, o_width = w_out.shape
    kv = k_width // HD
    heads = q_width // HD
    group = heads // kv
    nq = q_width // q_chunk
    no = o_width // o_chunk
    row_count, slot_count = key_cache.shape[0], key_cache.shape[1]
    h_rows = hidden.shape[0]
    gx_peers = [lax.rem(gx + k, n_gx) for k in range(1, n_gx)]
    yz_peers = [lax.rem(yz + k, n_yz) for k in range(1, n_yz)]

    def wq_copy(i):
        cols = pl.ds(pl.multiple_of(i * q_chunk, q_chunk), q_chunk)
        return pltpu.make_async_copy(
            w_query.at[:, cols], w_slots.at[i, pl.ds(0, depth), pl.ds(0, q_chunk)], wq_sem.at[i]
        )

    def wo_copy(i):
        cols = pl.ds(pl.multiple_of(i * o_chunk, o_chunk), o_chunk)
        return pltpu.make_async_copy(
            w_out.at[:, cols], w_slots.at[i, pl.ds(0, o_depth), pl.ds(0, o_chunk)], wo_sem.at[i]
        )

    def kc_copy(r):
        return pltpu.make_async_copy(key_cache.at[r], k_buf.at[r], kc_sem.at[r])

    def vc_copy(r):
        return pltpu.make_async_copy(value_cache.at[r], v_buf.at[r], vc_sem.at[r])

    x_own = pltpu.make_async_copy(hidden, x_all.at[yz], x_own_sem)
    x_own.start()
    barrier = pltpu.get_barrier_semaphore()
    for peer in yz_peers:
        pl.semaphore_signal(barrier, inc=1, device_id={"yz": peer}, device_id_type=MESH)
    for peer in gx_peers:
        pl.semaphore_signal(barrier, inc=1, device_id={"gx": peer}, device_id_type=MESH)
    wk_load = pltpu.make_async_copy(w_key, wk_buf, wkv_sem.at[0])
    wv_load = pltpu.make_async_copy(w_value, wv_buf, wkv_sem.at[1])
    wk_load.start()
    wv_load.start()
    for i in range(nq):
        wq_copy(i).start()
    pl.semaphore_wait(barrier, len(gx_peers) + len(yz_peers))

    def x_copy(peer, slot):
        return pltpu.make_async_remote_copy(
            src_ref=hidden,
            dst_ref=x_all.at[slot],
            send_sem=x_ssem.at[peer],
            recv_sem=x_rsem.at[slot],
            device_id={"yz": peer},
            device_id_type=MESH,
        )

    for peer in yz_peers:
        x_copy(peer, yz).start()
    x_own.wait()
    for peer in yz_peers:
        x_copy(peer, peer).wait_recv()

    step = min(depth, 512)
    squares = jnp.zeros((n_yz * h_rows, HD), F32)
    for at in range(0, depth, step):
        x = jnp.concatenate(
            [x_all[s, :, at : at + step].astype(F32) for s in range(n_yz)], axis=0
        )
        scaled[:, at : at + step] = (x * gain[:, at : at + step]).astype(BF16)
        sq = x * x
        for lane in range(0, step, HD):
            squares = squares + sq[:, lane : lane + HD]
    squares = jnp.broadcast_to(jnp.sum(squares, axis=1, keepdims=True), squares.shape)
    for d in range(n_gx):
        sq_own[d] = squares[d * row_count : (d + 1) * row_count]

    def sq_copy(peer, slot):
        return pltpu.make_async_remote_copy(
            src_ref=sq_own.at[peer],
            dst_ref=sq_recv.at[slot],
            send_sem=sq_ssem.at[peer],
            recv_sem=sq_rsem.at[slot],
            device_id={"gx": peer},
            device_id_type=MESH,
        )

    for peer in gx_peers:
        sq_copy(peer, gx).start()

    def p_copy(peer, slot, cols):
        return pltpu.make_async_remote_copy(
            src_ref=p_send.at[peer, :, cols],
            dst_ref=p_recv.at[slot, :, cols],
            send_sem=p_ssem.at[peer],
            recv_sem=p_rsem.at[slot],
            device_id={"gx": peer},
            device_id_type=MESH,
        )

    def project(weights, cols):
        y = jnp.dot(scaled[...], weights, preferred_element_type=F32)
        for d in range(n_gx):
            part = y[d * row_count : (d + 1) * row_count]
            p_own[d, :, cols] = part
            p_send[d, :, cols] = part.astype(BF16)
        for peer in gx_peers:
            p_copy(peer, gx, cols).start()

    wk_load.wait()
    project(wk_buf[...], pl.ds(q_width, k_width))
    wv_load.wait()
    project(wv_buf[...], pl.ds(q_width + k_width, k_width))

    def q_step(i, carry):
        wq_copy(i).wait()

        @pl.when(i == max(nq - 2, 0))
        def _():
            for r in range(row_count):
                kc_copy(r).start()
                vc_copy(r).start()

        cols = pl.ds(pl.multiple_of(i * q_chunk, q_chunk), q_chunk)
        project(w_slots[i, pl.ds(0, depth), pl.ds(0, q_chunk)], cols)
        return carry

    lax.fori_loop(0, nq, q_step, 0)
    early = min(2, no)
    for i in range(early):
        wo_copy(i).start()

    everything = pl.ds(0, q_width + 2 * k_width)
    sq_total = sq_own[gx]
    for peer in gx_peers:
        sq_copy(peer, peer).wait_recv()
        sq_total = sq_total + sq_recv[peer]
    inverse = lax.rsqrt(sq_total / D + 1e-05)
    for peer in gx_peers:
        p_copy(peer, peer, everything).wait_recv()
    cos, sin = cosine[...], sine[...]

    def summed(col):
        total = p_own[gx, :, col : col + HD]
        for peer in gx_peers:
            total = total + p_recv[peer, :, col : col + HD].astype(F32)
        return total * inverse

    def rope(v):
        return v * cos + pltpu.roll(v, HD // 2, 1) * sin

    for h in range(heads):
        q_rows[pl.ds(h, row_count, stride=heads), :] = rope(summed(h * HD))
    for g in range(kv):
        k_rows[pl.ds(g, row_count, stride=8), :] = rope(summed(q_width + g * HD))
        v_rows[pl.ds(g, row_count, stride=8), :] = summed(q_width + k_width + g * HD)

    def a_copy(peer, slot, r):
        return pltpu.make_async_remote_copy(
            src_ref=a_send.at[r],
            dst_ref=a_all.at[slot, r],
            send_sem=a_ssem.at[peer],
            recv_sem=a_rsem.at[slot],
            device_id={"gx": peer},
            device_id_type=MESH,
        )

    inv_root = HD ** (-0.5)

    def rounded(v):
        return v.astype(BF16).astype(F32)

    def spread(v):
        return jnp.concatenate(
            [jnp.broadcast_to(v[g : g + 1], (group, HD)) for g in range(kv)], axis=0
        )

    def row_step(r, carry):
        kc_copy(r).wait()

        if no > early:

            @pl.when(r + early < no)
            def _():
                wo_copy(jnp.minimum(r + early, no - 1)).start()

        q = rounded(q_rows[pl.ds(pl.multiple_of(r * heads, heads), heads), :])
        new_k = spread(rounded(k_rows[pl.ds(pl.multiple_of(r * 8, 8), 8), :]))
        new_v = spread(rounded(v_rows[pl.ds(pl.multiple_of(r * 8, 8), 8), :]))
        owner = lax.broadcasted_iota(jnp.int32, (heads, HD), 0) // group
        wide = jnp.concatenate(
            [jnp.where(owner == g, q, 0.0) for g in range(kv)], axis=1
        ).astype(BF16)
        scores = lax.dot_general(
            wide, k_buf[r], (((1,), (1,)), ((), ())), preferred_element_type=F32
        ) * inv_root
        fresh = jnp.sum(q * new_k, axis=1, keepdims=True) * inv_root
        slot = lax.broadcasted_iota(jnp.int32, (heads, slot_count), 1)
        masked = jnp.where(slot < lengths[r], scores, -jnp.inf)
        highest = jnp.maximum(jnp.max(masked, axis=1, keepdims=True), fresh)
        weights = jnp.exp(masked - highest)
        own = jnp.exp(fresh - highest)
        scale = 1.0 / (jnp.sum(weights, axis=1, keepdims=True) + own)
        probs = (weights * scale).astype(BF16)
        vc_copy(r).wait()
        mixed = jnp.dot(probs, v_buf[r], preferred_element_type=F32)
        mixed = jnp.concatenate(
            [
                mixed[g * group : (g + 1) * group, g * HD : (g + 1) * HD]
                for g in range(kv)
            ],
            axis=0,
        )
        mixed = (mixed + rounded(own * scale) * new_v).astype(BF16)
        a_send[r] = mixed
        a_all[gx, r] = mixed
        for peer in gx_peers:
            a_copy(peer, gx, r).start()
        return carry

    lax.fori_loop(0, row_count, row_step, 0)
    for i in range(row_count + early, no):
        wo_copy(i).start()

    def a_done(peer, slot):
        return pltpu.make_async_remote_copy(
            src_ref=a_send,
            dst_ref=a_all.at[slot],
            send_sem=a_ssem.at[peer],
            recv_sem=a_rsem.at[slot],
            device_id={"gx": peer},
            device_id_type=MESH,
        )

    for peer in gx_peers:
        a_done(peer, peer).wait_recv()
    span = row_count * heads
    for s in range(n_gx):
        for r in range(row_count):
            at = s * span + r * heads
            a_wide[at : at + heads, :] = a_all[s, r].astype(F32)
    for h in range(heads):
        attended[:, h * HD : (h + 1) * HD] = a_wide[
            pl.ds(h, n_gx * row_count, stride=heads), :
        ].astype(BF16)

    def o_copy(peer, slot, cols):
        return pltpu.make_async_remote_copy(
            src_ref=o_send.at[peer, :, cols],
            dst_ref=o_recv.at[slot, :, cols],
            send_sem=o_ssem.at[peer],
            recv_sem=o_rsem.at[slot],
            device_id={"yz": peer},
            device_id_type=MESH,
        )

    def o_step(i, carry):
        wo_copy(i).wait()
        cols = pl.ds(pl.multiple_of(i * o_chunk, o_chunk), o_chunk)
        y = jnp.dot(
            attended[...],
            w_slots[i, pl.ds(0, o_depth), pl.ds(0, o_chunk)],
            preferred_element_type=F32,
        )
        for d in range(n_yz):
            part = y[d * h_rows : (d + 1) * h_rows]
            o_own[d, :, cols] = part
            o_send[d, :, cols] = part.astype(BF16)
        for peer in yz_peers:
            o_copy(peer, yz, cols).start()
        return carry

    lax.fori_loop(0, no, o_step, 0)
    all_cols = pl.ds(0, o_width)
    for peer in yz_peers:
        o_copy(peer, peer, all_cols).wait_recv()
    for at in range(0, o_width, 512):
        total = x_all[yz, :, at : at + 512].astype(F32) + o_own[yz, :, at : at + 512]
        for peer in yz_peers:
            total = total + o_recv[peer, :, at : at + 512].astype(F32)
        out[:, at : at + 512] = total.astype(BF16)

    for peer in yz_peers:
        x_copy(peer, yz).wait_send()
        o_copy(peer, yz, all_cols).wait_send()
    for peer in gx_peers:
        sq_copy(peer, gx).wait_send()
        p_copy(peer, gx, everything).wait_send()
        a_done(peer, gx).wait_send()


def per_device(
    n_gx,
    n_yz,
    hidden,
    norm_gain,
    w_query,
    w_key,
    w_value,
    w_out,
    key_cache,
    value_cache,
    cache_lengths,
    positions,
):
    half = HD // 2
    counter = jnp.arange(half, dtype=F32)
    frequency = jnp.power(F32(500000.0), -2.0 * counter / HD)
    angles = positions.astype(F32)[:, None] * frequency[None, :]
    cosine, sine = jnp.cos(angles), jnp.sin(angles)
    cosine = jnp.concatenate([cosine, cosine], axis=1)
    sine = jnp.concatenate([-sine, sine], axis=1)
    gain = norm_gain.astype(F32)[None, :]

    h_rows = hidden.shape[0]
    depth, q_width = w_query.shape
    k_width = w_key.shape[1]
    o_depth, o_width = w_out.shape
    rows, slots, _ = key_cache.shape
    heads = q_width // HD
    q_chunk = min(512, q_width)
    o_chunk = min(512, o_width)
    nq, no = q_width // q_chunk, o_width // o_chunk
    all_rows = n_gx * rows
    p_width = q_width + 2 * k_width
    vmem = pl.BlockSpec(memory_space=pltpu.VMEM)
    smem = pl.BlockSpec(memory_space=pltpu.SMEM)
    anywhere = pl.BlockSpec(memory_space=pl.ANY)
    dma = pltpu.SemaphoreType.DMA
    return pl.pallas_call(
        functools.partial(kernel, n_gx, n_yz, q_chunk, o_chunk),
        out_shape=jax.ShapeDtypeStruct(hidden.shape, BF16),
        in_specs=[anywhere, vmem] + [anywhere] * 6 + [smem, vmem, vmem],
        out_specs=vmem,
        scratch_shapes=[
            pltpu.VMEM((max(nq, no), max(depth, o_depth), max(q_chunk, o_chunk)), BF16),
            pltpu.VMEM(w_key.shape, BF16),
            pltpu.VMEM(w_value.shape, BF16),
            pltpu.VMEM(key_cache.shape, BF16),
            pltpu.VMEM(value_cache.shape, BF16),
            pltpu.VMEM((n_yz, h_rows, depth), BF16),
            pltpu.VMEM((all_rows, depth), BF16),
            pltpu.VMEM((n_gx, rows, HD), F32),
            pltpu.VMEM((n_gx, rows, HD), F32),
            pltpu.VMEM((n_gx, rows, p_width), F32),
            pltpu.VMEM((n_gx, rows, p_width), BF16),
            pltpu.VMEM((n_gx, rows, p_width), BF16),
            pltpu.VMEM((rows * heads, HD), F32),
            pltpu.VMEM((rows * 8, HD), F32),
            pltpu.VMEM((rows * 8, HD), F32),
            pltpu.VMEM((rows, heads, HD), BF16),
            pltpu.VMEM((n_gx, rows, heads, HD), BF16),
            pltpu.VMEM((all_rows * heads, HD), F32),
            pltpu.VMEM((all_rows, o_depth), BF16),
            pltpu.VMEM((n_yz, h_rows, o_width), F32),
            pltpu.VMEM((n_yz, h_rows, o_width), BF16),
            pltpu.VMEM((n_yz, h_rows, o_width), BF16),
            dma((nq,)),
            dma((no,)),
            dma((2,)),
            dma((rows,)),
            dma((rows,)),
            dma,
            dma((n_yz,)),
            dma((n_yz,)),
            dma((n_gx,)),
            dma((n_gx,)),
            dma((n_gx,)),
            dma((n_gx,)),
            dma((n_gx,)),
            dma((n_gx,)),
            dma((n_yz,)),
            dma((n_yz,)),
        ],
        compiler_params=pltpu.CompilerParams(
            collective_id=0, has_side_effects=True, vmem_limit_bytes=62 * 2**20
        ),
    )(
        hidden,
        gain,
        w_query,
        w_key,
        w_value,
        w_out,
        key_cache,
        value_cache,
        cache_lengths,
        cosine,
        sine,
    )


def solution(mesh):
    in_specs = (
        P(("groups", "yz"), "gx"),
        P("gx"),
        P("gx", "yz"),
        P("gx", "yz"),
        P("gx", "yz"),
        P("yz", "gx"),
        P(("groups", "gx"), None, "yz"),
        P(("groups", "gx"), None, "yz"),
        P(("groups", "gx")),
        P(("groups", "gx")),
    )
    out_specs = P(("groups", "yz"), "gx")
    return jax.shard_map(
        functools.partial(per_device, mesh.shape["gx"], mesh.shape["yz"]),
        mesh=mesh,
        in_specs=in_specs,
        out_specs=out_specs,
        check_vma=False,
    )
```

time: 138 us -> 51.1 us (0.37)
  waiting for transfers between devices: 50.9 us -> 0 us
  Pallas kernels: 0 us -> 46.6 us
  matrix products: 39.6 us -> 0 us
  blocking collectives: 27.4 us -> 0 us
  between operations: 13.5 us -> 0.02 us
  other arithmetic: 6.35 us -> 2.76 us
    pallas_call x0 -> x1, Pallas kernels: none -> 46.6 us  [per_device(): pl.pallas_call(functools.partial(kernel, n_gx, n_yz, q_chunk, o_chunk), o...]
    dot_general x7 -> x0, matrix products: 39.6 us -> none  [the longest x1 14.5 us: per_device(): jnp.dot(all_rows, w_out, preferred_element_type=jnp.float32)]
    psum x1 -> x0, waiting for transfers between devices: 29 us -> none  [per_device(): summed, square_sum = lax.psum((partial_terms, squares), 'gx')]
    reduce_scatter x1 -> x0, waiting for transfers between devices: 21.8 us -> none  [per_device(): lax.psum_scatter(jnp.dot(all_rows, w_out, preferred_element_type=jnp.floa...]
    all_gather x2 -> x0, blocking collectives: 21.7 us -> none  [the longest x1 16 us: per_device(): gathered = lax.all_gather(hidden, 'yz', axis=0, tiled=True)]
    psum x1 -> x0, blocking collectives: 5.67 us -> none  [per_device(): summed, square_sum = lax.psum((partial_terms, squares), 'gx')]
    convert_element_type x5 -> x1, other arithmetic: 3.21 us -> 0.66 us  [per_device(): angles = positions.astype(F32)[:, None] * frequency[None, :]]
    unnamed x13 -> x1, local copies, waits for them, and re-layouts: 0.07 us -> 1.47 us
  transfers between devices with their start and end apart: 2 -> 0, of which waited for: 2 -> 0; matrix products, arithmetic and copies ran while one was open for 0% -> 0% of each run, Pallas kernels for 0% -> 0%
where the time goes in v1:
time: 51.1 us; the launch traced here: 50.9 us
  Pallas kernels  46.6 us (91%)
  other arithmetic  2.76 us (5%)
  local copies, waits for them, and re-layouts  1.47 us (3%)
    pallas_call x1, Pallas kernels, per_device(): pl.pallas_call(functools.partial(kernel, n_gx, n_yz, q_chunk, o_chunk), o...  46.6 us
    unnamed x1, local copies, waits for them, and re-layouts  1.47 us
    broadcast_in_dim x1, other arithmetic, per_device(): gain = norm_gain.astype(F32)[None, :]  1.3 us

profile of v1, /device:TPU:0, one launch (start us, length us, event | category | flops | bytes accessed | tf_op | source)
XLA Modules:
  0.0 50.9 jit_solution(11875222241261410316)
XLA Ops:
  0.0 0.7 %convert_element_type.4 = f32[8]{0:T(128)S(1)} convert(s32[8]{0:T(128)} %param.19) | non-fusion elementwise | flops 8 | bytes 64 | tf_op jit(solution)/shard_map/convert_element_type | solution.py:383
  0.7 0.1 fusion
  0.8 0.7 %pad_maximum_fusion = (f32[8,128]{1,0:T(8,128)}, f32[8,128]{1,0:T(8,128)}) fusion(f32[8,64]{1,0:T(8,128)S(1)} %get-tuple-element.7, f32[8,64]{1,0:T(8,128)S(1)} %get-tuple-element.6, f32[8,64]{1,0:T(8,128)S(1)} %get-tuple-element.5), kind=kLoop, calls=%fused_computation.2 | loop fusion | flops 2048 | bytes 14336 | tf_op jit(solution)/shard_map/concatenate | solution.py:385
  1.5 1.3 %broadcast_in_dim.9 = f32[4096]{0:T(1024)} convert(bf16[4096]{0:T(1024)(128)(2,1)} %param.11) | non-fusion elementwise | flops 4096 | bytes 24576 | tf_op jit(solution)/shard_map/broadcast_in_dim | solution.py:387
  2.8 46.6 %shard_map.100 = bf16[8,4096]{1,0:T(8,128)(2,1)} custom-call(bf16[8,4096]{1,0:T(8,128)(2,1)} %hidden.1, f32[1,4096]{1,0:T(1,128)} %bitcast.1, bf16[4096,4096]{1,0:T(8,128)(2,1)} %w_query.1, bf16[4096,256]{1,0:T(8,128)(2,1)} %w_key.1, bf16[4096,256]{1,0:T(8,128)(2,1)} %w_value.1, bf16[4096,4096]{1,0:T(8,128)(2,1)} %w_out.1, bf16[8,2048,256]{2,1,0:T(8,128)(2,1)} %key_cache.1, ...), custom_call_target="tpu_custom_call" | custom-call | tf_op jit(solution)/shard_map/pallas_call | solution.py:404
  49.4 1.5 %copy.12 = bf16[8,4096]{1,0:T(8,128)(2,1)} copy(bf16[8,4096]{1,0:T(8,128)(2,1)} %shard_map.100) | data formatting | bytes 131072
  (1 shorter events, 0.0 us)

commit v2 on v1

--- a/solution.py
+++ b/solution.py
@@ -14,23 +14,42 @@
 BF16 = jnp.bfloat16
 
 
+def tables(positions, rows):
+    half = HD // 2
+    row = lax.broadcasted_iota(jnp.int32, (rows, HD), 0)
+    lane = lax.broadcasted_iota(jnp.int32, (rows, HD), 1)
+    place = jnp.zeros((rows, HD), jnp.int32)
+    for r in range(rows):
+        place = jnp.where(row == r, positions[r], place)
+    frequency = jnp.zeros((rows, HD), F32)
+    for j in range(half):
+        value = 500000.0 ** (-2.0 * j / HD)
+        frequency = jnp.where(lane % half == j, value, frequency)
+    angle = place.astype(F32) * frequency
+    sine = jnp.sin(angle)
+    return jnp.cos(angle), jnp.where(lane < half, -sine, sine)
+
+
 def kernel(
     n_gx,
     n_yz,
     q_chunk,
     o_chunk,
     hidden,
-    gain,
+    norm_gain,
     w_query,
     w_key,
     w_value,
     w_out,
     key_cache,
     value_cache,
+    length_list,
+    position_list,
+    out,
+    gain,
     lengths,
-    cosine,
-    sine,
-    out,
+    positions,
+    small_sem,
     w_slots,
     wk_buf,
     wv_buf,
@@ -111,17 +130,28 @@
         pl.semaphore_signal(barrier, inc=1, device_id={"yz": peer}, device_id_type=MESH)
     for peer in gx_peers:
         pl.semaphore_signal(barrier, inc=1, device_id={"gx": peer}, device_id_type=MESH)
+    small = [
+        pltpu.make_async_copy(a, b, small_sem.at[i])
+        for i, (a, b) in enumerate(
+            [(norm_gain, gain), (length_list, lengths), (position_list, positions)]
+        )
+    ]
+    for load in small:
+        load.start()
     wk_load = pltpu.make_async_copy(w_key, wk_buf, wkv_sem.at[0])
     wv_load = pltpu.make_async_copy(w_value, wv_buf, wkv_sem.at[1])
     wk_load.start()
     wv_load.start()
     for i in range(nq):
-        wq_copy(i).start()
+        wq_copy(i).start(priority=1)
+    for r in range(row_count):
+        kc_copy(r).start(priority=1)
+        vc_copy(r).start(priority=1)
     pl.semaphore_wait(barrier, len(gx_peers) + len(yz_peers))
 
     def x_copy(peer, slot):
         return pltpu.make_async_remote_copy(
-            src_ref=hidden,
+            src_ref=x_all.at[yz],
             dst_ref=x_all.at[slot],
             send_sem=x_ssem.at[peer],
             recv_sem=x_rsem.at[slot],
@@ -129,22 +159,28 @@
             device_id_type=MESH,
         )
 
+    x_own.wait()
     for peer in yz_peers:
         x_copy(peer, yz).start()
-    x_own.wait()
+    for load in small:
+        load.wait()
+    cos, sin = tables(positions, row_count)
     for peer in yz_peers:
         x_copy(peer, peer).wait_recv()
 
     step = min(depth, 512)
+    gains = gain[...].astype(F32)
     squares = jnp.zeros((n_yz * h_rows, HD), F32)
     for at in range(0, depth, step):
         x = jnp.concatenate(
             [x_all[s, :, at : at + step].astype(F32) for s in range(n_yz)], axis=0
         )
-        scaled[:, at : at + step] = (x * gain[:, at : at + step]).astype(BF16)
         sq = x * x
         for lane in range(0, step, HD):
             squares = squares + sq[:, lane : lane + HD]
+            j = (at + lane) // HD
+            part = x[:, lane : lane + HD] * gains[j : j + 1]
+            scaled[:, at + lane : at + lane + HD] = part.astype(BF16)
     squares = jnp.broadcast_to(jnp.sum(squares, axis=1, keepdims=True), squares.shape)
     for d in range(n_gx):
         sq_own[d] = squares[d * row_count : (d + 1) * row_count]
@@ -189,20 +225,18 @@
     def q_step(i, carry):
         wq_copy(i).wait()
 
-        @pl.when(i == max(nq - 2, 0))
-        def _():
-            for r in range(row_count):
-                kc_copy(r).start()
-                vc_copy(r).start()
-
         cols = pl.ds(pl.multiple_of(i * q_chunk, q_chunk), q_chunk)
         project(w_slots[i, pl.ds(0, depth), pl.ds(0, q_chunk)], cols)
+
+        @pl.when(i < no)
+        def _():
+            wo_copy(jnp.minimum(i, no - 1)).start(priority=1)
+
         return carry
 
     lax.fori_loop(0, nq, q_step, 0)
-    early = min(2, no)
-    for i in range(early):
-        wo_copy(i).start()
+    for i in range(nq, no):
+        wo_copy(i).start(priority=1)
 
     everything = pl.ds(0, q_width + 2 * k_width)
     sq_total = sq_own[gx]
@@ -212,7 +246,6 @@
     inverse = lax.rsqrt(sq_total / D + 1e-05)
     for peer in gx_peers:
         p_copy(peer, peer, everything).wait_recv()
-    cos, sin = cosine[...], sine[...]
 
     def summed(col):
         total = p_own[gx, :, col : col + HD]
@@ -251,12 +284,6 @@
 
     def row_step(r, carry):
         kc_copy(r).wait()
-
-        if no > early:
-
-            @pl.when(r + early < no)
-            def _():
-                wo_copy(jnp.minimum(r + early, no - 1)).start()
 
         q = rounded(q_rows[pl.ds(pl.multiple_of(r * heads, heads), heads), :])
         new_k = spread(rounded(k_rows[pl.ds(pl.multiple_of(r * 8, 8), 8), :]))
@@ -292,10 +319,7 @@
             a_copy(peer, gx, r).start()
         return carry
 
-    lax.fori_loop(0, row_count, row_step, 0)
-    for i in range(row_count + early, no):
-        wo_copy(i).start()
-
+    lax.fori_loop(0, row_count, row_step, 0, unroll=True)
     def a_done(peer, slot):
         return pltpu.make_async_remote_copy(
             src_ref=a_send,
@@ -377,15 +401,7 @@
     cache_lengths,
     positions,
 ):
-    half = HD // 2
-    counter = jnp.arange(half, dtype=F32)
-    frequency = jnp.power(F32(500000.0), -2.0 * counter / HD)
-    angles = positions.astype(F32)[:, None] * frequency[None, :]
-    cosine, sine = jnp.cos(angles), jnp.sin(angles)
-    cosine = jnp.concatenate([cosine, cosine], axis=1)
-    sine = jnp.concatenate([-sine, sine], axis=1)
-    gain = norm_gain.astype(F32)[None, :]
-
+    gain = norm_gain.reshape(-1, HD)
     h_rows = hidden.shape[0]
     depth, q_width = w_query.shape
     k_width = w_key.shape[1]
@@ -398,15 +414,18 @@
     all_rows = n_gx * rows
     p_width = q_width + 2 * k_width
     vmem = pl.BlockSpec(memory_space=pltpu.VMEM)
-    smem = pl.BlockSpec(memory_space=pltpu.SMEM)
     anywhere = pl.BlockSpec(memory_space=pl.ANY)
     dma = pltpu.SemaphoreType.DMA
     return pl.pallas_call(
         functools.partial(kernel, n_gx, n_yz, q_chunk, o_chunk),
         out_shape=jax.ShapeDtypeStruct(hidden.shape, BF16),
-        in_specs=[anywhere, vmem] + [anywhere] * 6 + [smem, vmem, vmem],
+        in_specs=[anywhere] * 10,
         out_specs=vmem,
         scratch_shapes=[
+            pltpu.VMEM(gain.shape, BF16),
+            pltpu.SMEM(cache_lengths.shape, jnp.int32),
+            pltpu.SMEM(positions.shape, jnp.int32),
+            dma((3,)),
             pltpu.VMEM((max(nq, no), max(depth, o_depth), max(q_chunk, o_chunk)), BF16),
             pltpu.VMEM(w_key.shape, BF16),
             pltpu.VMEM(w_value.shape, BF16),
@@ -459,8 +478,7 @@
         key_cache,
         value_cache,
         cache_lengths,
-        cosine,
-        sine,
+        positions,
     )
 
 

time: 51.1 us -> 46.4 us (0.908)
  other arithmetic: 2.76 us -> 0 us
  Pallas kernels: 46.6 us -> 44.8 us
    pallas_call x1, Pallas kernels: 46.6 us -> 44.8 us  [per_device(): pl.pallas_call(functools.partial(kernel, n_gx, n_yz, q_chunk, o_chunk), o...]
    broadcast_in_dim x1 -> x0, other arithmetic: 1.3 us -> none  [per_device(): gain = norm_gain.astype(F32)[None, :]]
    concatenate x1 -> x0, other arithmetic: 0.68 us -> none  [per_device(): cosine = jnp.concatenate([cosine, cosine], axis=1)]
    convert_element_type x1 -> x0, other arithmetic: 0.66 us -> none  [per_device(): angles = positions.astype(F32)[:, None] * frequency[None, :]]
where the time goes in v2:
time: 46.4 us; the launch traced here: 46.3 us
  Pallas kernels  44.8 us (97%)
  local copies, waits for them, and re-layouts  1.47 us (3%)
    pallas_call x1, Pallas kernels, per_device(): pl.pallas_call(functools.partial(kernel, n_gx, n_yz, q_chunk, o_chunk), o...  44.8 us
    unnamed x1, local copies, waits for them, and re-layouts  1.47 us

profile of v2, /device:TPU:0, one launch (start us, length us, event | category | flops | bytes accessed | tf_op | source)
XLA Modules:
  0.0 46.3 jit_solution(12439066804753353141)
XLA Ops:
  0.0 44.8 %shard_map.100 = bf16[8,4096]{1,0:T(8,128)(2,1)} custom-call(bf16[8,4096]{1,0:T(8,128)(2,1)} %hidden.1, bf16[32,128]{1,0:T(8,128)(2,1)} %bitcast.1, bf16[4096,4096]{1,0:T(8,128)(2,1)} %w_query.1, bf16[4096,256]{1,0:T(8,128)(2,1)} %w_key.1, bf16[4096,256]{1,0:T(8,128)(2,1)} %w_value.1, bf16[4096,4096]{1,0:T(8,128)(2,1)} %w_out.1, ...), custom_call_target="tpu_custom_call" | custom-call | tf_op jit(solution)/shard_map/pallas_call | solution.py:419
  44.8 1.5 %copy.12 = bf16[8,4096]{1,0:T(8,128)(2,1)} copy(bf16[8,4096]{1,0:T(8,128)(2,1)} %shard_map.100) | data formatting | bytes 131072

commit v3 on v2

--- a/solution.py
+++ b/solution.py
@@ -368,7 +368,7 @@
             o_copy(peer, yz, cols).start()
         return carry
 
-    lax.fori_loop(0, no, o_step, 0)
+    lax.fori_loop(0, no, o_step, 0, unroll=2)
     all_cols = pl.ds(0, o_width)
     for peer in yz_peers:
         o_copy(peer, peer, all_cols).wait_recv()

time: 46.4 us -> 46.4 us (level)
  no operation moved by 1% of the time
where the time goes in v3:
time: 46.4 us; the launch traced here: 46.3 us
  Pallas kernels  44.8 us (97%)
  local copies, waits for them, and re-layouts  1.47 us (3%)
    pallas_call x1, Pallas kernels, per_device(): pl.pallas_call(functools.partial(kernel, n_gx, n_yz, q_chunk, o_chunk), o...  44.8 us
    unnamed x1, local copies, waits for them, and re-layouts  1.47 us

profile of v3, /device:TPU:0, one launch (start us, length us, event | category | flops | bytes accessed | tf_op | source)
XLA Modules:
  0.0 46.3 jit_solution(6891861563815575919)
XLA Ops:
  0.0 44.8 %shard_map.100 = bf16[8,4096]{1,0:T(8,128)(2,1)} custom-call(bf16[8,4096]{1,0:T(8,128)(2,1)} %hidden.1, bf16[32,128]{1,0:T(8,128)(2,1)} %bitcast.1, bf16[4096,4096]{1,0:T(8,128)(2,1)} %w_query.1, bf16[4096,256]{1,0:T(8,128)(2,1)} %w_key.1, bf16[4096,256]{1,0:T(8,128)(2,1)} %w_value.1, bf16[4096,4096]{1,0:T(8,128)(2,1)} %w_out.1, ...), custom_call_target="tpu_custom_call" | custom-call | tf_op jit(solution)/shard_map/pallas_call | solution.py:419
  44.8 1.5 %copy.12 = bf16[8,4096]{1,0:T(8,128)(2,1)} copy(bf16[8,4096]{1,0:T(8,128)(2,1)} %shard_map.100) | data formatting | bytes 131072
